TPU v7x, 32 devices: a whole 2x2x4 slice. The times are simulated.
32 devices in a mesh: req: 8 (over z, y), mlp: 4 (over x, core).
Axes of the slice: x: 2, y: 2, z: 4, core: 2. Of those that a mesh axis runs over, the one named last changes fastest.
Arguments:
- residual: bfloat16 [2048, 2048], P('req'), may hold values from -20 to 20
- query_rows: bfloat16 [2048, 2048], P('req', 'mlp'), may hold values from -6 to 6
- value_rows: bfloat16 [2048, 2048], P('req', 'mlp'), may hold values from -6 to 6
- forget_logit: float32 [2048, 2048], P('req', 'mlp'), may hold values from 0 to 40
- slot_kind: int32 [2048], P('req'), may hold values from 0 to 2, as said below
- head_gain: float32 [2048], P('mlp'), may hold values from 0.1 to 1.9
- out_weight: bfloat16 [2048, 2048], P('mlp', 'req'), may hold values from -0.125 to 0.125
- ffn_gain: float32 [2048], replicated, may hold values from 0.1 to 1.9
- gate_weight: bfloat16 [2048, 3072], P('req', 'mlp'), may hold values from -0.125 to 0.125
- up_weight: bfloat16 [2048, 3072], P('req', 'mlp'), may hold values from -0.125 to 0.125
- down_weight: bfloat16 [3072, 2048], P('mlp', 'req'), may hold values from -0.109375 to 0.109375
Outputs:
- layer_out: bfloat16 [2048, 2048], P('req', 'mlp')
Inputs may be any that keep to these rules, and one draw needn't show every extreme that they name: `slot_kind`: slots 0 to 1535 hold one prompt: slot 0 has kind 2, the others kind 1. Every other block of 256 slots holds short requests packed from its first slot, then empty slots; a short request has at most 32 tokens, the first request of each such block exactly 32. Over all 2048 slots exactly 1664 are live.
All inputs are finite; a program needn't handle non-finite values.
Results may differ from a plain program's by a relative error of at most 0.0163.
Values may be sent and summed in bfloat16 or wider, within the bound.
A program may use at most 128 MiB of HBM per device.

v0:
```python
import jax
import jax.numpy as jnp
from jax import lax
from jax.sharding import PartitionSpec as P

HEAD = 128
SPAN = 32


def carried_in(part, axis, combine, identity):
    place = lax.axis_index(axis)
    gathered = jax.tree.map(lambda a: lax.all_gather(a, axis), part)
    state = jax.tree.map(lambda a, e: jnp.zeros_like(a) + jnp.asarray(e, a.dtype), part, identity)

    def one(hop, state):
        return combine(
            state, jax.tree.map(lambda a: lax.dynamic_index_in_dim(a, hop, 0, False), gathered)
        )

    return lax.fori_loop(0, place, one, state)


def span_step(passed_state, pieces):
    query_block, key_block, value_block, g_block = pieces
    top_precision = lax.Precision.HIGHEST
    inside_block_term = jnp.cumsum(g_block, axis=0)
    between_blocks_term = jnp.einsum(
        "owu,wuj->owj",
        query_block * jnp.exp(inside_block_term),
        passed_state,
        precision=top_precision,
    )
    length = g_block.shape[0]
    causal = jnp.arange(length)[:, None] >= jnp.arange(length)[None, :]
    causal = causal[:, :, None, None]
    gap_log = jnp.where(causal, inside_block_term[:, None] - inside_block_term[None, :], 0.0)
    decay_pairs = jnp.where(causal, jnp.exp(gap_log), 0.0)
    scores = jnp.einsum(
        "tnk,tsnk->tsn", query_block, decay_pairs * key_block[None], precision=top_precision
    )
    intra_part = jnp.einsum("tsn,snv->tnv", scores, value_block, precision=top_precision)
    final_decay_sum = inside_block_term[-1]
    updated_state = jnp.exp(final_decay_sum)[:, :, None] * passed_state + jnp.einsum(
        "weq,wel->eql",
        key_block * jnp.exp(final_decay_sum[None] - inside_block_term),
        value_block,
        precision=top_precision,
    )
    return (updated_state, between_blocks_term + intra_part)


def compose(earlier, later):
    return (
        earlier[0] * later[0],
        later[0][:, :, None] * earlier[1] + later[1],
        earlier[2] + later[2],
    )


def on_device(
    residual,
    query_rows,
    value_rows,
    forget_logit,
    slot_kind,
    head_gain,
    out_weight,
    ffn_gain,
    gate_weight,
    up_weight,
    down_weight,
):
    slot_total = residual.shape[0]
    quarter = query_rows.shape[1]
    heads_here = quarter // HEAD
    live_mask = slot_kind > 0
    first_mask = slot_kind == 2
    log_forget = jnp.where(
        first_mask[:, None],
        -80.0,
        jnp.where(live_mask[:, None], -jax.nn.softplus(-forget_logit), 0.0),
    )
    key_gate = jnp.where(live_mask[:, None], jax.nn.sigmoid(-forget_logit), 0.0)
    shape4 = (slot_total // SPAN, SPAN, heads_here, HEAD)
    q_all = query_rows.astype(jnp.float32).reshape(shape4)
    v_all = value_rows.astype(jnp.float32).reshape(shape4)
    k_all = key_gate.reshape(shape4)
    g_all = log_forget.reshape(shape4)
    zero_state = jnp.zeros((heads_here, HEAD, HEAD), jnp.float32)
    decay_whole = jnp.exp(jnp.sum(log_forget, axis=0)).reshape(heads_here, HEAD)
    live_count = jnp.sum(live_mask.astype(jnp.float32))
    neutral = (jnp.ones_like(decay_whole), jnp.zeros_like(zero_state), jnp.zeros((), jnp.float32))
    end_state, local_out = lax.scan(span_step, zero_state, (q_all, k_all, v_all, g_all))
    leading_decay = carried_in((decay_whole, end_state, live_count), "req", compose, neutral)
    within_all = jnp.cumsum(g_all, axis=1)
    block_total = within_all[:, -1]
    before_block = jnp.cumsum(block_total, axis=0) - block_total
    query_damped = q_all * jnp.exp(within_all + before_block[:, None])
    heads_out = local_out + jnp.einsum(
        "mosf,sfl->mosl", query_damped, leading_decay[1], precision=lax.Precision.HIGHEST
    )
    heads_out = heads_out.reshape(slot_total, heads_here, HEAD)
    mean_sq = jnp.mean(heads_out * heads_out, axis=-1, keepdims=True)
    head_normed = (
        heads_out / jnp.sqrt(mean_sq + 1e-06) * head_gain.reshape(heads_here, HEAD)
    ).astype(jnp.bfloat16)
    head_normed = head_normed.reshape(slot_total, quarter)
    partial_rows = jnp.dot(
        head_normed,
        lax.all_gather(out_weight, "req", axis=1, tiled=True),
        preferred_element_type=jnp.float32,
    )
    mixed_sum = lax.psum(partial_rows.astype(jnp.bfloat16), "mlp").astype(jnp.float32)
    stream = (residual.astype(jnp.float32) + mixed_sum).astype(jnp.bfloat16)
    my_cols = lax.axis_index("mlp") * quarter
    rows_f = stream.astype(jnp.float32)
    ffn_in = (
        rows_f / jnp.sqrt(jnp.mean(rows_f * rows_f, axis=-1, keepdims=True) + 1e-05) * ffn_gain
    ).astype(jnp.bfloat16)
    gate_acc = jnp.dot(
        ffn_in,
        lax.all_gather(gate_weight, "req", axis=0, tiled=True),
        preferred_element_type=jnp.float32,
    )
    up_acc = jnp.dot(
        ffn_in,
        lax.all_gather(up_weight, "req", axis=0, tiled=True),
        preferred_element_type=jnp.float32,
    )
    hidden = (jax.nn.silu(gate_acc) * up_acc).astype(jnp.bfloat16)
    terms = jnp.dot(
        hidden,
        lax.all_gather(down_weight, "req", axis=1, tiled=True),
        preferred_element_type=jnp.float32,
    )
    ffn_out = lax.psum_scatter(
        terms.astype(jnp.bfloat16), "mlp", scatter_dimension=1, tiled=True
    ).astype(jnp.float32)
    own_cols = lax.dynamic_slice_in_dim(stream, my_cols, quarter, 1).astype(jnp.float32)
    result = (own_cols + ffn_out).astype(jnp.bfloat16)
    layer_out = jnp.where(live_mask[:, None], result, jnp.zeros_like(result))
    return layer_out


def solution(mesh):
    return jax.shard_map(
        on_device,
        mesh=mesh,
        in_specs=(
            P("req", None),
            P("req", "mlp"),
            P("req", "mlp"),
            P("req", "mlp"),
            P("req"),
            P("mlp"),
            P("mlp", "req"),
            P(),
            P("req", "mlp"),
            P("req", "mlp"),
            P("mlp", "req"),
        ),
        out_specs=P("req", "mlp"),
        check_vma=False,
    )
```

profile of v0, /device:TPU:24, one launch (start us, length us, event | category | flops | bytes accessed | tf_op | source)
XLA Modules:
  0.0 427.1 jit_solution(12621466244140202450)
XLA Ops:
  7.3 1.6 fusion.38
  9.6 50.4 %while.27 = (s32[]{:T(128)}, f32[4,128,128]{2,1,0:T(8,128)S(1)}, f32[8,32,4,128]{3,1,0,2:T(8,128)S(1)}, f32[8,32,4,128]{3,2,1,0:T(4,128)S(1)}, f32[8,32,4,128]{3...) while((s32[]{:T(128)}, f32[4,128,128]{2,1,0:T(8,128)S(1)}, ...), condition=%wide.region_2.3_spmd.clone, body=%wide.region_0.2_spmd.clone.sunk | while | flops 65848320 | bytes 6453368 | solution.py:93
  9.7 1.6 select_multiply_fusion.2
  11.3 3.3 fusion.68
  16.0 1.6 select_multiply_fusion.2
  17.6 3.3 fusion.68
  22.3 1.6 select_multiply_fusion.2
  23.9 3.3 fusion.68
  28.6 1.6 select_multiply_fusion.2
  30.2 3.3 fusion.68
  34.9 1.6 select_multiply_fusion.2
  36.5 3.3 fusion.68
  41.2 1.6 select_multiply_fusion.2
  42.8 3.3 fusion.68
  47.5 1.6 select_multiply_fusion.2
  49.1 3.3 fusion.68
  53.8 1.6 select_multiply_fusion.2
  55.4 3.3 fusion.68
  62.4 22.4 %all_gather.23 = f32[8,4,128]{2,1,0:T(4,128)S(1)} all-gather(f32[1,4,128]{2,1,0:T(4,128)S(1)} %exponential_bitcast_fusion), channel_id=1, replica_groups=mesh['req'=8,'mlp'=4] {'req'}, dimensions={0}, use_global_device_ids=true | all-gather | bytes 18432 | tf_op jit(solution)/shard_map/all_gather | solution.py:12
  84.9 24.8 %all-gather.15.cloned.1.call-done = f32[32,128,128]{2,1,0:T(8,128)} async-done(((f32[4,128,128]{2,1,0:T(8,128)}), f32[32,128,128]{2,1,0:T(8,128)}) %all-gather.15.cloned.1.call-update) | async-done | bytes 2097168 | tf_op jit(solution)/shard_map/all_gather | solution.py:12
  109.7 7.0 %while.26 = (s32[]{:T(128)}, f32[4,128,128]{2,1,0:T(8,128)S(1)}, s32[]{:T(128)}, f32[8,4,128]{2,1,0:T(4,128)S(1)}, f32[8,4,128,128]{3,2,1,0:T(8,128)}, /*index=5*/s32[]{:T(128)}, s32[]{:T(128)}, s32[]{:T(128)}) while((s32[]{:T(128)}, f32[4,128,128]{2,1,0:T(8,128)S(1)}, s32[]{:T(128)}, f32[8,4,128]{2,1,0:T(4,128)S(1)}, ...), condition=%wide.region_5.6_spmd, body=%wide.region_4.5_spmd.sunk | while | flops 131077 | bytes 792703 | solution.py:20
  118.0 42.9 %all-gather.7.cloned.1.call-done = bf16[512,2048]{1,0:T(8,128)(2,1)} async-done(((bf16[512,256]{1,0:T(8,128)(2,1)}), bf16[512,2048]{1,0:T(8,128)(2,1)}) %all-gather.7.cloned.1.call-update) | async-done | bytes 2097168 | tf_op jit(solution)/shard_map/all_gather | solution.py:110
  161.3 3.3 convolution_convert_fusion
  166.4 34.5 %all-reduce.2.cloned.1.call-done = bf16[256,2048]{1,0:T(8,128)(2,1)} async-done(((bf16[256,2048]{1,0:T(8,128)(2,1)}), bf16[256,2048]{1,0:T(8,128)(2,1)}) %all-reduce.2.cloned.1.call-update) | async-done | bytes 1048592 | tf_op jit(solution)/shard_map/psum | solution.py:113
  200.9 1.7 fusion.18
  202.6 60.0 %all-gather.9.cloned.1.call-done = bf16[2048,768]{1,0:T(8,128)(2,1)} async-done(((bf16[256,768]{1,0:T(8,128)(2,1)}), bf16[2048,768]{1,0:T(8,128)(2,1)}) %all-gather.9.cloned.1.call-update) | async-done | bytes 3145744 | tf_op jit(solution)/shard_map/all_gather | solution.py:122
  262.6 2.9 fusion.36
  265.6 58.4 %all-gather.11.cloned.1.call-done = bf16[2048,768]{1,0:T(8,128)(2,1)} async-done(((bf16[256,768]{1,0:T(8,128)(2,1)}), bf16[2048,768]{1,0:T(8,128)(2,1)}) %all-gather.11.cloned.1.call-update) | async-done | bytes 3145744 | tf_op jit(solution)/shard_map/all_gather | solution.py:127
  324.0 63.3 %all-gather.13.cloned.1.call-done = bf16[768,2048]{1,0:T(8,128)(2,1)} async-done(((bf16[768,256]{1,0:T(8,128)(2,1)}), bf16[768,2048]{1,0:T(8,128)(2,1)}) %all-gather.13.cloned.1.call-update) | async-done | bytes 3145744 | tf_op jit(solution)/shard_map/all_gather | solution.py:133
  387.3 6.1 %convolution_convert_fusion.1 = bf16[256,2048]{1,0:T(8,128)(2,1)} fusion(bf16[768,2048]{1,0:T(8,128)(2,1)} %all-gather.13.cloned.1.call-done, bf16[2048,768]{1,0:T(8,128)(2,1)} %all-gather.11.cloned.1.call-done, f32[256,768]{1,0:T(8,128)S(1)} %fusion.36, bf16[256,2048]{1,0:T(8,128)(2,1)S(1)} %get-tuple-element.172, f32[2048]{0:T(1024)S(1)} %copy-done.4, ...), kind=kOutput, calls=%fused_computation.35 | convolution fusion | flops 1614413824 | bytes 9184256 | tf_op jit(solution)/shard_map/dot_general | solution.py:131
  393.4 25.1 %reduce-scatter.2.cloned.1.call-done = bf16[256,512]{1,0:T(8,128)(2,1)} async-done(((bf16[256,2048]{1,0:T(8,128)(2,1)}), bf16[256,512]{1,0:T(8,128)(2,1)}) %reduce-scatter.2.cloned.1.call-update) | async-done | bytes 262160 | tf_op jit(solution)/shard_map/reduce_scatter | solution.py:136
  418.5 1.8 fusion.30
  (132 shorter events, 24.5 us)
Async XLA Ops:
  6.5 2.5 copy-start.2
  6.5 103.1 %all-gather.15.cloned.1.call-start = ((), (), s32[]{:S(2)}) async-start(), calls=%async_computation.7 | async-start | bytes 2359296 | tf_op jit(solution)/shard_map/all_gather | solution.py:12
  7.3 2.1 copy-start.3
  60.0 0.7 copy-start
  60.7 100.2 %all-gather.7.cloned.1.call-start = ((), (), s32[]{:S(2)}) async-start(), calls=%async_computation.1 | async-start | bytes 2359296 | tf_op jit(solution)/shard_map/all_gather | solution.py:110
  61.4 139.4 %all-reduce.2.cloned.1.call-start = ((), (), s32[]{:S(2)}) async-start(), calls=%async_computation.2 | async-start | bytes 2097152 | tf_op jit(solution)/shard_map/psum | solution.py:113
  116.7 44.6 %copy-start.5 = (f32[512]{0:T(512)S(1)}, f32[512]{0:T(512)}, u32[]{:S(2)}) copy-start(f32[512]{0:T(512)} %param.20) | copy-start | bytes 6148
  164.6 36.3 %copy-start.1 = (bf16[256,2048]{1,0:T(8,128)(2,1)S(1)}, bf16[256,2048]{1,0:T(8,128)(2,1)}, u32[]{:S(2)}) copy-start(bf16[256,2048]{1,0:T(8,128)(2,1)} %param.15) | copy-start | bytes 3145732
  164.6 98.0 %copy-start.4 = (f32[2048]{0:T(1024)S(1)}, f32[2048]{0:T(1024)}, u32[]{:S(2)}) copy-start(f32[2048]{0:T(1024)} %param.22) | copy-start | bytes 24580
  164.6 98.0 %all-gather.9.cloned.1.call-start = ((), (), s32[]{:S(2)}) async-start(), calls=%async_computation.3 | async-start | bytes 3538944 | tf_op jit(solution)/shard_map/all_gather | solution.py:122
  165.2 158.8 %all-gather.11.cloned.1.call-start = ((), (), s32[]{:S(2)}) async-start(), calls=%async_computation.4 | async-start | bytes 3538944 | tf_op jit(solution)/shard_map/all_gather | solution.py:127
  165.8 221.5 %all-gather.13.cloned.1.call-start = ((), (), s32[]{:S(2)}) async-start(), calls=%async_computation.5 | async-start | bytes 3538944 | tf_op jit(solution)/shard_map/all_gather | solution.py:133
  166.3 252.2 %reduce-scatter.2.cloned.1.call-start = ((), (), s32[]{:S(2)}) async-start(), calls=%async_computation.6 | async-start | bytes 1310720 | tf_op jit(solution)/shard_map/reduce_scatter | solution.py:136
Sparse Core Ops, SparseCore 0:
  60.8 48.8 all-gather.14
  111.7 49.1 all-gather.6
  164.7 36.1 all-reduce.1
  203.1 59.4 all-gather.8
  264.9 59.0 all-gather.10
  326.1 61.1 all-gather.12
  393.5 24.9 reduce-scatter.1
where the time goes:
time: 429 us; the launch traced here: 427 us
  waiting for transfers between devices  311 us (72%)
  matrix products  49.2 us (11%)
  other arithmetic  26.9 us (6%)
  blocking collectives  22.4 us (5%)
  between operations  13.7 us (3%)
    all_gather x1, waiting for transfers between devices, on_device(): lax.all_gather(down_weight, 'req', axis=1, tiled=True)  63.3 us
    all_gather x1, waiting for transfers between devices, on_device(): lax.all_gather(gate_weight, 'req', axis=0, tiled=True)  60 us
    all_gather x1, waiting for transfers between devices, on_device(): lax.all_gather(up_weight, 'req', axis=0, tiled=True)  58.4 us
    all_gather x1, waiting for transfers between devices, on_device(): lax.all_gather(out_weight, 'req', axis=1, tiled=True)  42.9 us
    psum x1, waiting for transfers between devices, on_device(): lax.psum(partial_rows.astype(jnp.bfloat16), 'mlp').astype(jnp.float32)  34.5 us
    dot_general x8, matrix products, span_step(): jnp.einsum('tnk,tsnk->tsn', query_block, decay_pairs * key_block[None], p...  26.8 us
    reduce_scatter x1, waiting for transfers between devices, on_device(): lax.psum_scatter(terms.astype(jnp.bfloat16), 'mlp', scatter_dimension=1,...  25.1 us
    all_gather x1, waiting for transfers between devices, carried_in(): gathered = jax.tree.map(lambda a: lax.all_gather(a, axis), part)  24.8 us
  transfers between devices with their start and end apart: 7, of which 7 were waited for; matrix products, arithmetic and copies ran while one was open for 3% of the time, Pallas kernels for 0%

commit v1 on v0

--- a/solution.py
+++ b/solution.py
@@ -1,6 +1,8 @@
 import jax
 import jax.numpy as jnp
 from jax import lax
+from jax.experimental import pallas as pl
+from jax.experimental.pallas import tpu as pltpu
 from jax.sharding import PartitionSpec as P
 
 HEAD = 128
@@ -94,7 +96,11 @@
     leading_decay = carried_in((decay_whole, end_state, live_count), "req", compose, neutral)
     within_all = jnp.cumsum(g_all, axis=1)
     block_total = within_all[:, -1]
-    before_block = jnp.cumsum(block_total, axis=0) - block_total
+    blocks = block_total.shape[0]
+    earlier = (jnp.arange(blocks)[:, None] > jnp.arange(blocks)[None, :]).astype(jnp.float32)
+    before_block = jnp.einsum(
+        "mb,bnk->mnk", earlier, block_total, precision=lax.Precision.HIGHEST
+    )
     query_damped = q_all * jnp.exp(within_all + before_block[:, None])
     heads_out = local_out + jnp.einsum(
         "mosf,sfl->mosl", query_damped, leading_decay[1], precision=lax.Precision.HIGHEST
@@ -142,9 +148,422 @@
     return layer_out
 
 
+CHUNK = 64
+LINE = 4
+PAIR = 2
+GROUPS = 4
+MESH = pl.DeviceIdType.MESH
+NT = (((1,), (1,)), ((), ()))
+TN = (((0,), (0,)), ((), ()))
+NN = (((1,), (0,)), ((), ()))
+
+
+def mm(a, b, dims=NN):
+    return lax.dot_general(a, b, dims, preferred_element_type=jnp.float32)
+
+
+def layer_kernel(
+    residual_far, query_hbm, value_hbm, logit_hbm, kind_row, head_gain, ffn_gain,
+    w_out, w_gate, w_up, w_down,
+    out,
+    residual, query, value, logit, alive,
+    g_out, g_gate, g_up, g_down,
+    heads_sum, query_far, state, state_out, state_in, decay_out, decay_in,
+    normed, part, part_in, stream, ffn_in, hidden, term, term_in,
+    load_sem, own_sem, send_sem, recv_sem, st_send, st_recv, dc_send, dc_recv, mx_send, mx_recv,
+):
+    f32, bf16 = jnp.float32, jnp.bfloat16
+    me = lax.axis_index("req")
+    grp = lax.axis_index("mlp")
+    n_req = LINE * PAIR
+    z = me // PAIR
+    y = me % PAIR
+    mate = me + 1 - 2 * y
+    slots, quarter = query.shape
+    heads = quarter // HEAD
+    own = (w_out, w_gate, w_up, w_down)
+    held = (g_out, g_gate, g_up, g_down)
+    pieces = range(4)
+
+    loads = [
+        pltpu.make_async_copy(src, dst, load_sem.at[i])
+        for i, (src, dst) in enumerate(
+            ((logit_hbm, logit), (query_hbm, query), (value_hbm, value), (residual_far, residual))
+        )
+    ]
+    keeps = [
+        pltpu.make_async_copy(own[p], held[p].at[me], own_sem.at[p]) for p in pieces
+    ]
+    for copy in loads + keeps:
+        copy.start()
+
+    barrier = pltpu.get_barrier_semaphore()
+    for d in range(1, n_req):
+        pl.semaphore_signal(barrier, inc=1, device_id={"req": (me + d) % n_req}, device_id_type=MESH)
+    for d in range(1, GROUPS):
+        pl.semaphore_signal(barrier, inc=1, device_id={"mlp": (grp + d) % GROUPS}, device_id_type=MESH)
+    pl.semaphore_wait(barrier, n_req - 1 + GROUPS - 1)
+
+    def hop(p, slot, way, src=None):
+        target = (mate, me + PAIR, me - PAIR)[way]
+        return pltpu.make_async_remote_copy(
+            src_ref=held[p].at[slot] if src is None else src,
+            dst_ref=held[p].at[slot],
+            send_sem=send_sem.at[p, slot, way],
+            recv_sem=recv_sem.at[p, slot],
+            device_id={"req": target},
+            device_id_type=MESH,
+        )
+
+    def landed(p, slot):
+        hop(p, slot, 0).wait_recv()
+
+    def send_own(p):
+        @pl.when(z < LINE - 1)
+        def _():
+            hop(p, me, 1, own[p]).start()
+
+        @pl.when(z > 0)
+        def _():
+            hop(p, me, 2, own[p]).start()
+
+        hop(p, me, 0, own[p]).start()
+
+    def relay(p, slot, way):
+        landed(p, slot)
+
+        @pl.when(z < LINE - 1 if way == 1 else z > 0)
+        def _():
+            hop(p, slot, way).start()
+
+        if p > 0:
+            hop(p, slot, 0).start()
+
+    def forward(p, k):
+        if k == 0:
+            landed(0, mate)
+
+            @pl.when(z < LINE - 1)
+            def _():
+                hop(0, mate, 1).start()
+
+            @pl.when(z > 0)
+            def _():
+                hop(0, mate, 2).start()
+
+            return
+
+        @pl.when(z >= k)
+        def _():
+            relay(p, me - PAIR * k, 1)
+            if p == 0:
+                relay(p, mate - PAIR * k, 1)
+
+        @pl.when(z + k < LINE)
+        def _():
+            relay(p, me + PAIR * k, 2)
+            if p == 0:
+                relay(p, mate + PAIR * k, 2)
+
+    def complete(p):
+        for j in range(LINE):
+            landed(p, PAIR * j + 1 - y)
+
+    for p in (0, 1, 2):
+        send_own(p)
+
+    state[...] = jnp.zeros_like(state)
+    rows_i = lax.broadcasted_iota(jnp.int32, (CHUNK, CHUNK), 0)
+    cols_i = lax.broadcasted_iota(jnp.int32, (CHUNK, CHUNK), 1)
+    lower = jnp.where(rows_i >= cols_i, 1.0, 0.0).astype(f32)
+    upper = jnp.where(rows_i <= cols_i, 1.0, 0.0).astype(f32)
+    ones = jnp.ones((CHUNK, CHUNK), bf16)
+    before = jnp.zeros((1, quarter), f32)
+    same = jnp.where(rows_i == cols_i, 1.0, 0.0).astype(f32)
+    across = jnp.ones((CHUNK, quarter), bf16)
+    for copy in loads[:3]:
+        copy.wait()
+    for c in range(slots // CHUNK):
+        rows = pl.ds(c * CHUNK, CHUNK)
+        kinds = mm((same * kind_row[c : c + 1, :].astype(f32)).astype(bf16), across)
+        live = kinds > 0.5
+        alive[rows, :] = kinds
+        first_c = jnp.where(kinds[:, :CHUNK] > 1.5, 1.0, 0.0).astype(f32)
+        first_r = jnp.where(kind_row[c : c + 1, :] == 2, 1.0, 0.0).astype(f32)
+        small = jnp.exp(-logit[rows, :])
+        plain = live & (kinds < 1.5)
+        g = jnp.where(plain, -jnp.log1p(small), 0.0)
+        key = jnp.where(live, small / (1.0 + small), 0.0)
+        inner = lax.dot_general(lower, g, NN, precision=lax.Precision.HIGHEST, preferred_element_type=f32)
+        count_t = mm((lower * first_r).astype(bf16), ones)
+        count_s = mm(ones, (upper * first_c).astype(bf16))
+        reset = jnp.where(rows_i >= cols_i, jnp.exp(-80.0 * jnp.maximum(count_t - count_s, 0.0)), 0.0)
+        whole = inner - 80.0 * count_t[:, 0:1]
+        last = whole[CHUNK - 1 : CHUNK, :]
+        q = query[rows, :].astype(f32)
+        v = value[rows, :]
+        q_in = (q * jnp.exp(inner)).astype(bf16)
+        k_in = (key * jnp.exp(-inner)).astype(bf16)
+        q_old = (q * jnp.exp(whole)).astype(bf16)
+        k_end = (key * jnp.exp(last - whole)).astype(bf16)
+        query_far[rows, :] = (q * jnp.exp(whole + before)).astype(bf16)
+        keep = jnp.exp(last)
+        before = before + last
+        for h in range(heads):
+            cols = slice(h * HEAD, (h + 1) * HEAD)
+            scores = (mm(q_in[:, cols], k_in[:, cols], NT) * reset).astype(bf16)
+            old = state[:, cols]
+            heads_sum[rows, cols] = mm(scores, v[:, cols]) + mm(q_old[:, cols], old.astype(bf16), NT)
+            state[:, cols] = keep[:, cols] * old + mm(v[:, cols], k_end[:, cols], TN)
+        if c == 0:
+            forward(0, 0)
+        if c == 1:
+            send_own(3)
+        if c == 2:
+            forward(0, 1)
+
+    state_out[...] = state[...].astype(bf16)
+    decay_out[...] = jnp.broadcast_to(jnp.exp(before), decay_out.shape)
+
+    def to_later(d, slot, target):
+        return (
+            pltpu.make_async_remote_copy(
+                src_ref=state_out, dst_ref=state_in.at[slot], send_sem=st_send.at[d],
+                recv_sem=st_recv.at[slot], device_id={"req": target}, device_id_type=MESH,
+            ),
+            pltpu.make_async_remote_copy(
+                src_ref=decay_out, dst_ref=decay_in.at[slot], send_sem=dc_send.at[d],
+                recv_sem=dc_recv.at[slot], device_id={"req": target}, device_id_type=MESH,
+            ),
+        )
+
+    for d in range(1, n_req):
+        @pl.when(me + d < n_req)
+        def _(d=d):
+            for copy in to_later(d, me, me + d):
+                copy.start()
+
+    forward(1, 1)
+    forward(2, 1)
+    forward(0, 2)
+    forward(3, 1)
+
+    state[...] = jnp.zeros_like(state)
+
+    def carry(u, _):
+        for copy in to_later(0, u, mate):
+            copy.wait_recv()
+        state[...] = decay_in[u][0:1, :] * state[...] + state_in[u].astype(f32)
+        return 0
+
+    lax.fori_loop(0, me, carry, 0)
+    forward(0, 3)
+    for h in range(heads):
+        cols = slice(h * HEAD, (h + 1) * HEAD)
+        o = heads_sum[:, cols] + mm(query_far[:, cols], state[:, cols].astype(bf16), NT)
+        mean_sq = jnp.mean(o * o, axis=-1, keepdims=True)
+        normed[:, cols] = (o / jnp.sqrt(mean_sq + 1e-06) * head_gain[:, cols]).astype(bf16)
+    forward(1, 2)
+    forward(2, 2)
+    for copy in keeps + loads[3:]:
+        copy.wait()
+
+    wide = w_out.shape[1]
+    per = n_req // GROUPS
+    for r in range(n_req):
+        at = slice((r % per) * wide, (r % per + 1) * wide)
+        part[r // per, :, at] = mm(normed[...], g_out[r]).astype(bf16)
+
+    def to_group(step, src, dst, slot, target):
+        return pltpu.make_async_remote_copy(
+            src_ref=src, dst_ref=dst, send_sem=mx_send.at[step, target],
+            recv_sem=mx_recv.at[step, slot], device_id={"mlp": target}, device_id_type=MESH,
+        )
+
+    def exchange(step, source, into):
+        copies = []
+        for d in range(1, GROUPS):
+            other = (grp + d) % GROUPS
+            copy = to_group(step, source(other), into.at[grp], d, other)
+            copy.start()
+            copies.append(copy)
+        return copies
+
+    first = exchange(0, lambda j: part.at[j], part_in)
+    forward(3, 2)
+    my_part = part[grp].astype(f32)
+    for copy in first:
+        copy.wait_recv()
+    total = my_part
+    for d in range(1, GROUPS):
+        total = total + part_in[(grp + d) % GROUPS].astype(f32)
+    mine = residual[:, pl.ds(pl.multiple_of(grp * quarter, quarter), quarter)]
+    stream[grp] = (mine.astype(f32) + total).astype(bf16)
+    second = exchange(1, lambda j: stream.at[grp], stream)
+    forward(1, 3)
+    forward(2, 3)
+    for copy in second:
+        copy.wait_recv()
+    square = jnp.zeros((slots, 1), f32)
+    for j in range(GROUPS):
+        s = stream[j].astype(f32)
+        square = square + jnp.sum(s * s, axis=-1, keepdims=True)
+    width = quarter * GROUPS
+    scale = jnp.sqrt(square / width + 1e-05)
+    for j in range(GROUPS):
+        ffn_in[j] = (stream[j].astype(f32) / scale * ffn_gain[j : j + 1, :]).astype(bf16)
+    complete(1)
+    complete(2)
+    deep = w_gate.shape[0]
+    gate = jnp.zeros((slots, w_gate.shape[1]), f32)
+    up = jnp.zeros((slots, w_gate.shape[1]), f32)
+    for r in range(n_req):
+        x = ffn_in[r // per, :, (r % per) * deep : (r % per + 1) * deep]
+        gate = gate + mm(x, g_gate[r])
+        up = up + mm(x, g_up[r])
+    hidden[...] = (gate / (1.0 + jnp.exp(-gate)) * up).astype(bf16)
+
+    def down(j):
+        landed(3, PAIR * j + 1 - y)
+        for i in range(PAIR):
+            at = slice(i * wide, (i + 1) * wide)
+            term[j, :, at] = mm(hidden[...], g_down[PAIR * j + i]).astype(bf16)
+
+        @pl.when(grp != j)
+        def _():
+            to_group(2, term.at[j], term_in.at[grp], grp, j).start()
+
+    down(z)
+    for k in range(1, LINE):
+        if k == LINE - 1:
+            forward(3, k)
+
+        @pl.when(z >= k)
+        def _(k=k):
+            down(z - k)
+
+        @pl.when(z + k < LINE)
+        def _(k=k):
+            down(z + k)
+
+    total = term[grp].astype(f32)
+    for d in range(1, GROUPS):
+        other = (grp + d) % GROUPS
+        to_group(2, term.at[other], term_in.at[other], other, other).wait_recv()
+        total = total + term_in[other].astype(f32)
+    result = (stream[grp].astype(f32) + total).astype(bf16)
+    out[...] = jnp.where(alive[...] > 0.5, result, jnp.zeros_like(result))
+
+    for copy in first + second:
+        copy.wait_send()
+    for d in range(1, GROUPS):
+        other = (grp + d) % GROUPS
+        to_group(2, term.at[other], term_in.at[grp], grp, other).wait_send()
+    for d in range(1, n_req):
+        @pl.when(me + d < n_req)
+        def _(d=d):
+            for copy in to_later(d, me, me + d):
+                copy.wait_send()
+    def sent(p, slot, up, down, over):
+        if over:
+            hop(p, slot, 0).wait_send()
+        if up:
+            @pl.when(z < LINE - 1)
+            def _():
+                hop(p, slot, 1).wait_send()
+        if down:
+            @pl.when(z > 0)
+            def _():
+                hop(p, slot, 2).wait_send()
+
+    for p in pieces:
+        sent(p, me, True, True, True)
+        if p == 0:
+            sent(p, mate, True, True, False)
+        for k in range(1, LINE):
+            @pl.when(z >= k)
+            def _(p=p, k=k):
+                sent(p, me - PAIR * k, True, False, p > 0)
+                if p == 0:
+                    sent(p, mate - PAIR * k, True, False, False)
+
+            @pl.when(z + k < LINE)
+            def _(p=p, k=k):
+                sent(p, me + PAIR * k, False, True, p > 0)
+                if p == 0:
+                    sent(p, mate + PAIR * k, False, True, False)
+
+
+def in_one_kernel(
+    residual, query_rows, value_rows, forget_logit, slot_kind, head_gain,
+    out_weight, ffn_gain, gate_weight, up_weight, down_weight,
+):
+    f32, bf16 = jnp.float32, jnp.bfloat16
+    slots, quarter = query_rows.shape
+    n_req = LINE * PAIR
+    dma = pltpu.SemaphoreType.DMA
+    vmem = pltpu.VMEM
+    cube = (GROUPS, slots, quarter)
+    return pl.pallas_call(
+        layer_kernel,
+        out_shape=jax.ShapeDtypeStruct((slots, quarter), bf16),
+        in_specs=[pl.BlockSpec(memory_space=pltpu.HBM)] * 4
+        + [pl.BlockSpec(memory_space=pltpu.VMEM)] * 3
+        + [pl.BlockSpec(memory_space=pltpu.HBM)] * 4,
+        out_specs=pl.BlockSpec(memory_space=pltpu.VMEM),
+        scratch_shapes=[
+            vmem(residual.shape, bf16),
+            vmem((slots, quarter), bf16),
+            vmem((slots, quarter), bf16),
+            vmem((slots, quarter), f32),
+            vmem((slots, quarter), f32),
+            vmem((n_req, *out_weight.shape), bf16),
+            vmem((n_req, *gate_weight.shape), bf16),
+            vmem((n_req, *up_weight.shape), bf16),
+            vmem((n_req, *down_weight.shape), bf16),
+            vmem((slots, quarter), f32),
+            vmem((slots, quarter), bf16),
+            vmem((HEAD, quarter), f32),
+            vmem((HEAD, quarter), bf16),
+            vmem((n_req, HEAD, quarter), bf16),
+            vmem((8, quarter), f32),
+            vmem((n_req, 8, quarter), f32),
+            vmem((slots, quarter), bf16),
+            vmem(cube, bf16),
+            vmem(cube, bf16),
+            vmem(cube, bf16),
+            vmem(cube, bf16),
+            vmem((slots, gate_weight.shape[1]), bf16),
+            vmem(cube, bf16),
+            vmem(cube, bf16),
+            dma((4,)),
+            dma((4,)),
+            dma((4, n_req, 3)),
+            dma((4, n_req)),
+            dma((n_req,)),
+            dma((n_req,)),
+            dma((n_req,)),
+            dma((n_req,)),
+            dma((3, GROUPS)),
+            dma((3, GROUPS)),
+        ],
+        compiler_params=pltpu.CompilerParams(
+            collective_id=0, has_side_effects=True, vmem_limit_bytes=50 << 20
+        ),
+        cost_estimate=pl.CostEstimate(flops=6 << 30, bytes_accessed=16 << 20, transcendentals=1 << 20),
+    )(
+        residual,
+        query_rows, value_rows, forget_logit,
+        slot_kind.reshape(slots // CHUNK, CHUNK),
+        head_gain.reshape(1, quarter), ffn_gain.reshape(GROUPS, quarter),
+        out_weight, gate_weight, up_weight, down_weight,
+    )
+
+
 def solution(mesh):
+    fits = mesh.shape["req"] == LINE * PAIR and mesh.shape["mlp"] == GROUPS
     return jax.shard_map(
-        on_device,
+        in_one_kernel if fits else on_device,
         mesh=mesh,
         in_specs=(
             P("req", None),

time: 429 us -> 172 us (0.40)
  waiting for transfers between devices: 311 us -> 0 us
  Pallas kernels: 0 us -> 161 us
  matrix products: 49.2 us -> 0 us
  other arithmetic: 26.9 us -> 0 us
  blocking collectives: 22.4 us -> 0 us
  between operations: 13.7 us -> 0.02 us
  local copies, waits for them, and re-layouts: 2.56 us -> 10.3 us
    all_gather x5 -> x0, waiting for transfers between devices: 249 us -> none  [the longest x1 63.3 us: on_device(): lax.all_gather(down_weight, 'req', axis=1, tiled=True)]
    pallas_call x0 -> x1, Pallas kernels: none -> 161 us  [in_one_kernel(): pl.pallas_call(layer_kernel, out_shape=jax.ShapeDtypeStruct((slots, quart...]
    dot_general x35 -> x0, matrix products: 48.6 us -> none  [the longest x8 26.8 us: span_step(): jnp.einsum('tnk,tsnk->tsn', query_block, decay_pairs * key_block[None], p...]
    psum x1 -> x0, waiting for transfers between devices: 34.5 us -> none  [on_device(): lax.psum(partial_rows.astype(jnp.bfloat16), 'mlp').astype(jnp.float32)]
    reduce_scatter x1 -> x0, waiting for transfers between devices: 25.1 us -> none  [on_device(): lax.psum_scatter(terms.astype(jnp.bfloat16), 'mlp', scatter_dimension=1,...]
    all_gather x1 -> x0, blocking collectives: 22.4 us -> none  [carried_in(): gathered = jax.tree.map(lambda a: lax.all_gather(a, axis), part)]
    mul x17 -> x0, other arithmetic: 13.3 us -> none  [the longest x8 12.5 us: span_step(): decay_pairs * key_block[None]]
    unnamed x12 -> x21, local copies, waits for them, and re-layouts: 0.72 us -> 9.49 us
  transfers between devices with their start and end apart: 7 -> 0, of which waited for: 7 -> 0; matrix products, arithmetic and copies ran while one was open for 3% -> 0% of each run, Pallas kernels for 0% -> 0%
where the time goes in v1:
time: 172 us; the launch traced here: 171 us
  Pallas kernels  161 us (94%)
  local copies, waits for them, and re-layouts  10.3 us (6%)
    pallas_call x1, Pallas kernels, in_one_kernel(): pl.pallas_call(layer_kernel, out_shape=jax.ShapeDtypeStruct((slots, quart...  161 us
    unnamed x21, local copies, waits for them, and re-layouts  9.49 us

profile of v1, /device:TPU:24, one launch (start us, length us, event | category | flops | bytes accessed | tf_op | source)
XLA Modules:
  0.0 171.4 jit_solution(9338695222981612228)
XLA Ops:
  0.0 0.0 copy-start.9
  0.0 0.7 copy-done.9
  0.7 0.1 reshape.9.kind_row
  0.8 0.0 copy-start.8
  0.8 0.7 reshape.11.ffn_gain
  1.5 0.0 copy-done.8
  1.5 0.0 copy-start
  1.5 1.2 copy-done
  2.7 0.0 copy-start.1
  2.7 1.0 copy-done.1
  3.8 0.0 copy-start.2
  3.8 1.0 copy-done.2
  4.7 0.0 copy-start.3
  4.8 1.0 copy-done.3
  5.7 0.0 copy-start.4
  5.7 1.0 copy-done.4
  6.7 0.0 copy-start.5
  6.7 0.9 copy-done.5
  7.7 0.0 copy-start.6
  7.7 0.9 copy-done.6
  8.6 0.0 copy-start.7
  8.6 0.9 copy-done.7
  9.6 161.1 %shard_map.109 = bf16[256,512]{1,0:T(8,128)(2,1)S(1)} custom-call(bf16[256,2048]{1,0:T(8,128)(2,1)S(1)} %copy-done, bf16[256,512]{1,0:T(8,128)(2,1)S(1)} %copy-done.5, bf16[256,512]{1,0:T(8,128)(2,1)S(1)} %copy-done.6, f32[256,512]{1,0:T(8,128)S(1)} %copy-done.1, s32[4,64]{1,0:T(4,128)S(1)} %reshape.9.kind_row, f32[1,512]{1,0:T(1,128)S(1)} %bitcast.1, ...), custom_call_target="tpu_custom_call" | custom-call | flops 6442450944 | bytes 16777216 | tf_op jit(solution)/shard_map/pallas_call | solution.py:507
  170.7 0.7 copy.13
Async XLA Ops:
  0.0 0.7 copy-start.9
  0.8 0.7 copy-start.8
  1.5 1.2 copy-start
  2.7 1.0 copy-start.1
  3.8 1.0 copy-start.2
  4.7 1.0 copy-start.3
  5.7 1.0 copy-start.4
  6.7 0.9 copy-start.5
  7.7 0.9 copy-start.6
  8.6 0.9 copy-start.7

commit v2 on v1

--- a/solution.py
+++ b/solution.py
@@ -168,7 +168,7 @@
     out,
     residual, query, value, logit, alive,
     g_out, g_gate, g_up, g_down,
-    heads_sum, query_far, state, state_out, state_in, decay_out, decay_in,
+    heads_sum, query_far, state, state_out, state_pair, state_in, decay_out, decay_pair, decay_in,
     normed, part, part_in, stream, ffn_in, hidden, term, term_in,
     load_sem, own_sem, send_sem, recv_sem, st_send, st_recv, dc_send, dc_recv, mx_send, mx_recv,
 ):
@@ -181,9 +181,25 @@
     mate = me + 1 - 2 * y
     slots, quarter = query.shape
     heads = quarter // HEAD
-    own = (w_out, w_gate, w_up, w_down)
-    held = (g_out, g_gate, g_up, g_down)
-    pieces = range(4)
+    half_out, half_down = w_out.shape[0] // 2, w_down.shape[0] // 2
+    table = (
+        (w_out, g_out, 0, half_out),
+        (w_gate, g_gate, 0, w_gate.shape[0]),
+        (w_up, g_up, 0, w_up.shape[0]),
+        (w_down, g_down, 0, half_down),
+        (w_out, g_out, half_out, half_out),
+        (w_down, g_down, half_down, half_down),
+    )
+    pieces = range(len(table))
+
+    def own(p):
+        shard, _, start, count = table[p]
+        return shard.at[pl.ds(start, count), :]
+
+    def held(p, slot):
+        _, gathered, start, count = table[p]
+        return gathered.at[slot, pl.ds(start, count), :]
+
 
     loads = [
         pltpu.make_async_copy(src, dst, load_sem.at[i])
@@ -192,7 +208,7 @@
         )
     ]
     keeps = [
-        pltpu.make_async_copy(own[p], held[p].at[me], own_sem.at[p]) for p in pieces
+        pltpu.make_async_copy(own(p), held(p, me), own_sem.at[p]) for p in pieces
     ]
     for copy in loads + keeps:
         copy.start()
@@ -207,8 +223,8 @@
     def hop(p, slot, way, src=None):
         target = (mate, me + PAIR, me - PAIR)[way]
         return pltpu.make_async_remote_copy(
-            src_ref=held[p].at[slot] if src is None else src,
-            dst_ref=held[p].at[slot],
+            src_ref=held(p, slot) if src is None else src,
+            dst_ref=held(p, slot),
             send_sem=send_sem.at[p, slot, way],
             recv_sem=recv_sem.at[p, slot],
             device_id={"req": target},
@@ -221,13 +237,13 @@
     def send_own(p):
         @pl.when(z < LINE - 1)
         def _():
-            hop(p, me, 1, own[p]).start()
+            hop(p, me, 1, own(p)).start()
 
         @pl.when(z > 0)
         def _():
-            hop(p, me, 2, own[p]).start()
-
-        hop(p, me, 0, own[p]).start()
+            hop(p, me, 2, own(p)).start()
+
+        hop(p, me, 0, own(p)).start()
 
     def relay(p, slot, way):
         landed(p, slot)
@@ -269,7 +285,7 @@
         for j in range(LINE):
             landed(p, PAIR * j + 1 - y)
 
-    for p in (0, 1, 2):
+    for p in (0, 4, 1, 2):
         send_own(p)
 
     state[...] = jnp.zeros_like(state)
@@ -319,52 +335,76 @@
             forward(0, 0)
         if c == 1:
             send_own(3)
+            send_own(5)
         if c == 2:
             forward(0, 1)
+            forward(4, 1)
 
     state_out[...] = state[...].astype(bf16)
     decay_out[...] = jnp.broadcast_to(jnp.exp(before), decay_out.shape)
 
-    def to_later(d, slot, target):
+    def pass_on(src, decay, d, slot, target):
         return (
             pltpu.make_async_remote_copy(
-                src_ref=state_out, dst_ref=state_in.at[slot], send_sem=st_send.at[d],
+                src_ref=src, dst_ref=state_in.at[slot], send_sem=st_send.at[d],
                 recv_sem=st_recv.at[slot], device_id={"req": target}, device_id_type=MESH,
             ),
             pltpu.make_async_remote_copy(
-                src_ref=decay_out, dst_ref=decay_in.at[slot], send_sem=dc_send.at[d],
+                src_ref=decay, dst_ref=decay_in.at[slot], send_sem=dc_send.at[d],
                 recv_sem=dc_recv.at[slot], device_id={"req": target}, device_id_type=MESH,
             ),
         )
 
-    for d in range(1, n_req):
-        @pl.when(me + d < n_req)
-        def _(d=d):
-            for copy in to_later(d, me, me + d):
+    to_mate = pass_on(state_out, decay_out, 0, LINE, mate)
+    for copy in to_mate:
+        copy.start()
+    forward(1, 1)
+    for copy in to_mate:
+        copy.wait_recv()
+    d_own, s_own = decay_out[...], state[...]
+    d_mate, s_mate = decay_in[LINE], state_in[LINE].astype(f32)
+    early = y == 0
+    state_pair[...] = (
+        jnp.where(early, s_own, s_mate) * jnp.where(early, d_mate, d_own)[0:1, :]
+        + jnp.where(early, s_mate, s_own)
+    ).astype(bf16)
+    decay_pair[...] = d_own * d_mate
+    for k in range(1, LINE):
+        @pl.when(z + k < LINE)
+        def _(k=k):
+            for copy in pass_on(state_pair, decay_pair, k, z, me + PAIR * k):
                 copy.start()
 
-    forward(1, 1)
     forward(2, 1)
     forward(0, 2)
+    forward(4, 2)
     forward(3, 1)
+    forward(5, 1)
+    forward(1, 2)
+    forward(2, 2)
 
     state[...] = jnp.zeros_like(state)
 
     def carry(u, _):
-        for copy in to_later(0, u, mate):
+        for copy in pass_on(state_pair, decay_pair, 0, u, mate):
             copy.wait_recv()
         state[...] = decay_in[u][0:1, :] * state[...] + state_in[u].astype(f32)
         return 0
 
-    lax.fori_loop(0, me, carry, 0)
+    lax.fori_loop(0, z, carry, 0)
+
+    @pl.when(y == 1)
+    def _():
+        state[...] = decay_in[LINE][0:1, :] * state[...] + state_in[LINE].astype(f32)
+
     forward(0, 3)
+    forward(4, 3)
     for h in range(heads):
         cols = slice(h * HEAD, (h + 1) * HEAD)
         o = heads_sum[:, cols] + mm(query_far[:, cols], state[:, cols].astype(bf16), NT)
         mean_sq = jnp.mean(o * o, axis=-1, keepdims=True)
         normed[:, cols] = (o / jnp.sqrt(mean_sq + 1e-06) * head_gain[:, cols]).astype(bf16)
-    forward(1, 2)
-    forward(2, 2)
+    complete(4)
     for copy in keeps + loads[3:]:
         copy.wait()
 
@@ -391,6 +431,7 @@
 
     first = exchange(0, lambda j: part.at[j], part_in)
     forward(3, 2)
+    forward(5, 2)
     my_part = part[grp].astype(f32)
     for copy in first:
         copy.wait_recv()
@@ -425,6 +466,7 @@
 
     def down(j):
         landed(3, PAIR * j + 1 - y)
+        landed(5, PAIR * j + 1 - y)
         for i in range(PAIR):
             at = slice(i * wide, (i + 1) * wide)
             term[j, :, at] = mm(hidden[...], g_down[PAIR * j + i]).astype(bf16)
@@ -437,6 +479,7 @@
     for k in range(1, LINE):
         if k == LINE - 1:
             forward(3, k)
+            forward(5, k)
 
         @pl.when(z >= k)
         def _(k=k):
@@ -459,10 +502,12 @@
     for d in range(1, GROUPS):
         other = (grp + d) % GROUPS
         to_group(2, term.at[other], term_in.at[grp], grp, other).wait_send()
-    for d in range(1, n_req):
-        @pl.when(me + d < n_req)
-        def _(d=d):
-            for copy in to_later(d, me, me + d):
+    for copy in to_mate:
+        copy.wait_send()
+    for k in range(1, LINE):
+        @pl.when(z + k < LINE)
+        def _(k=k):
+            for copy in pass_on(state_pair, decay_pair, k, z, me + PAIR * k):
                 copy.wait_send()
     def sent(p, slot, up, down, over):
         if over:
@@ -525,9 +570,11 @@
             vmem((slots, quarter), bf16),
             vmem((HEAD, quarter), f32),
             vmem((HEAD, quarter), bf16),
-            vmem((n_req, HEAD, quarter), bf16),
+            vmem((HEAD, quarter), bf16),
+            vmem((LINE + 1, HEAD, quarter), bf16),
             vmem((8, quarter), f32),
-            vmem((n_req, 8, quarter), f32),
+            vmem((8, quarter), f32),
+            vmem((LINE + 1, 8, quarter), f32),
             vmem((slots, quarter), bf16),
             vmem(cube, bf16),
             vmem(cube, bf16),
@@ -537,18 +584,18 @@
             vmem(cube, bf16),
             vmem(cube, bf16),
             dma((4,)),
-            dma((4,)),
-            dma((4, n_req, 3)),
-            dma((4, n_req)),
-            dma((n_req,)),
-            dma((n_req,)),
-            dma((n_req,)),
-            dma((n_req,)),
+            dma((6,)),
+            dma((6, n_req, 3)),
+            dma((6, n_req)),
+            dma((LINE,)),
+            dma((LINE + 1,)),
+            dma((LINE,)),
+            dma((LINE + 1,)),
             dma((3, GROUPS)),
             dma((3, GROUPS)),
         ],
         compiler_params=pltpu.CompilerParams(
-            collective_id=0, has_side_effects=True, vmem_limit_bytes=50 << 20
+            collective_id=0, has_side_effects=True, vmem_limit_bytes=60 << 20
         ),
         cost_estimate=pl.CostEstimate(flops=6 << 30, bytes_accessed=16 << 20, transcendentals=1 << 20),
     )(

time: 172 us -> 148 us (0.86)
  Pallas kernels: 161 us -> 143 us
  local copies, waits for them, and re-layouts: 10.3 us -> 4.31 us
    pallas_call x1, Pallas kernels: 161 us -> 143 us  [in_one_kernel(): pl.pallas_call(layer_kernel, out_shape=jax.ShapeDtypeStruct((slots, quart...]
    unnamed x21 -> x3, local copies, waits for them, and re-layouts: 9.49 us -> 2.35 us
where the time goes in v2:
time: 148 us; the launch traced here: 147 us
  Pallas kernels  143 us (97%)
  local copies, waits for them, and re-layouts  4.31 us (3%)
    pallas_call x1, Pallas kernels, in_one_kernel(): pl.pallas_call(layer_kernel, out_shape=jax.ShapeDtypeStruct((slots, quart...  143 us

profile of v2, /device:TPU:24, one launch (start us, length us, event | category | flops | bytes accessed | tf_op | source)
XLA Modules:
  0.0 147.3 jit_solution(3371760261184552819)
XLA Ops:
  0.0 0.0 copy-start
  0.0 0.7 copy-done
  0.7 0.7 reshape.9.kind_row
  1.3 1.3 reshape.11.ffn_gain
  2.6 143.0 %shard_map.109 = bf16[256,512]{1,0:T(8,128)(2,1)} custom-call(bf16[256,2048]{1,0:T(8,128)(2,1)} %residual_far.1, bf16[256,512]{1,0:T(8,128)(2,1)} %query_hbm.1, bf16[256,512]{1,0:T(8,128)(2,1)} %value_hbm.1, f32[256,512]{1,0:T(8,128)} %logit_hbm.1, s32[4,64]{1,0:T(4,128)} %reshape.9.kind_row, f32[1,512]{1,0:T(1,128)} %bitcast.1, f32[4,512]{1,0:T(4,128)} %reshape.11.ffn_gain, ...), custom_call_target="tpu_custom_call" | custom-call | flops 6442450944 | bytes 16777216 | tf_op jit(solution)/shard_map/pallas_call | solution.py:552
  145.6 1.7 %copy.13 = bf16[256,512]{1,0:T(8,128)(2,1)} copy(bf16[256,512]{1,0:T(8,128)(2,1)} %shard_map.109) | data formatting | bytes 524288
Async XLA Ops:
  0.0 0.7 copy-start
